TPU v7x, 32 devices: a whole 2x2x4 slice. The times are simulated.
32 devices in a mesh: parts: 1, loop: 32 (over z, y, x, core).
Axes of the slice: x: 2, y: 2, z: 4, core: 2. Of those that a mesh axis runs over, the one named last changes fastest.
Arguments:
- slots: bfloat16 [2048, 4096], P(('parts', 'loop')), may hold values from -6 to 6
- tile_expert: int32 [16, 1], P('parts'), may hold values from 0 to 1
- slot_weight: float32 [2048], P(('parts', 'loop')), may hold values from 0.2 to 1
- gate_weight: bfloat16 [2, 4096, 12288], P(None, None, 'loop'), may hold values from -0.09375 to 0.09375
- up_weight: bfloat16 [2, 4096, 12288], P(None, None, 'loop'), may hold values from -0.09375 to 0.09375
- down_weight: bfloat16 [2, 12288, 4096], P(None, 'loop'), may hold values from -0.0546875 to 0.0546875
Outputs:
- expert_out: bfloat16 [2048, 4096], P(('parts', 'loop'))
Inputs may be any that keep to these rules, and one draw needn't show every extreme that they name: `tile_expert`: each block names one expert; every expert is named by some block.
All inputs are finite; a program needn't handle non-finite values.
Results may differ from a plain program's by a relative error of at most 0.0049.
Values may be sent and summed in bfloat16 or wider, within the bound.
A program may use at most 256 MiB of HBM per device.

v0:
```python
import jax
import jax.numpy as jnp
from jax import lax
from jax.sharding import PartitionSpec as P

TILE = 128


def expert_part(row_block, chosen, gate_weight, up_weight, down_weight):
    gate_cols = lax.dynamic_index_in_dim(gate_weight, chosen, 0, keepdims=False)
    up_cols = lax.dynamic_index_in_dim(up_weight, chosen, 0, keepdims=False)
    down_rows = lax.dynamic_index_in_dim(down_weight, chosen, 0, keepdims=False)
    gate_value = jnp.dot(row_block, gate_cols, preferred_element_type=jnp.float32)
    up_value = jnp.dot(row_block, up_cols, preferred_element_type=jnp.float32)
    hidden = (jax.nn.silu(gate_value) * up_value).astype(jnp.bfloat16)
    return jnp.dot(hidden, down_rows, preferred_element_type=jnp.float32)


def per_device(slots, tile_expert, slot_weight, gate_weight, up_weight, down_weight):
    chosen_ids = tile_expert[:, 0]
    width = slots.shape[1]
    gathered = lax.all_gather(slots, "loop", axis=0, tiled=True)
    tile_rows = gathered.reshape(-1, TILE, width)

    def expert_tile(operands):
        row_block, chosen = operands
        return expert_part(row_block, chosen, gate_weight, up_weight, down_weight)

    partial_value = lax.map(expert_tile, (tile_rows, chosen_ids)).reshape(-1, width)
    summed = lax.psum_scatter(partial_value, "loop", scatter_dimension=0, tiled=True)
    return (slot_weight[:, None] * summed).astype(jnp.bfloat16)


def solution(mesh):
    in_specs = (
        P(("parts", "loop"), None),
        P("parts", None),
        P(("parts", "loop")),
        P(None, None, "loop"),
        P(None, None, "loop"),
        P(None, "loop", None),
    )
    out_specs = P(("parts", "loop"), None)
    return jax.shard_map(
        per_device, mesh=mesh, in_specs=in_specs, out_specs=out_specs, check_vma=False
    )
```

profile of v0, /device:TPU:0, one launch (start us, length us, event | category | flops | bytes accessed | tf_op | source)
XLA Modules:
  0.0 680.1 jit_solution(9170488530532572225)
XLA Ops:
  7.3 120.5 %all-gather.2.cloned.1.call-done = bf16[2048,4096]{1,0:T(8,128)(2,1)} async-done(((bf16[64,4096]{1,0:T(8,128)(2,1)}), bf16[2048,4096]{1,0:T(8,128)(2,1)}) %all-gather.2.cloned.1.call-update) | async-done | bytes 16777232 | tf_op jit(solution)/shard_map/all_gather | solution.py:22
  127.8 190.7 %while.10 = (s32[]{:T(128)}, f32[16,128,4096]{2,1,0:T(8,128)}, bf16[16,128,4096]{2,1,0:T(8,128)(2,1)}, s32[16]{0:T(128)}, bf16[2,4096,384]{2,1,0:T(8,128)(2,1)},...) while((s32[]{:T(128)}, f32[16,128,4096]{2,1,0:T(8,128)}, ...), condition=%wide.region_1.2_spmd, body=%wide.region_0.1_spmd.sunk | while | flops 1208254464 | bytes 14027415 | solution.py:29
  130.9 2.9 fusion.45
  133.8 5.9 fusion.46
  142.8 2.9 fusion.45
  145.8 5.9 fusion.46
  154.7 2.9 fusion.45
  157.7 5.9 fusion.46
  166.6 2.9 fusion.45
  169.6 5.9 fusion.46
  178.6 2.9 fusion.45
  181.5 5.9 fusion.46
  190.5 2.9 fusion.45
  193.5 5.9 fusion.46
  202.4 2.9 fusion.45
  205.4 5.9 fusion.46
  214.4 2.9 fusion.45
  217.3 5.9 fusion.46
  229.2 5.9 fusion.46
  241.1 5.8 fusion.46
  253.0 5.9 fusion.46
  262.0 2.9 fusion.45
  264.9 5.9 fusion.46
  273.9 2.9 fusion.45
  276.9 5.9 fusion.46
  285.9 2.9 fusion.45
  288.8 5.9 fusion.46
  297.8 2.9 fusion.45
  300.7 5.9 fusion.46
  309.7 2.9 fusion.45
  312.6 5.9 fusion.46
  318.5 352.6 %reduce-scatter.2.cloned.1.call-done = f32[64,4096]{1,0:T(8,128)} async-done(((f32[2048,4096]{1,0:T(8,128)}), f32[64,4096]{1,0:T(8,128)}) %reduce-scatter.2.cloned.1.call-update) | async-done | bytes 1048592 | tf_op jit(solution)/shard_map/reduce_scatter | solution.py:30
  (27 shorter events, 31.6 us)
Async XLA Ops:
  6.5 121.3 %all-gather.2.cloned.1.call-start = ((), (), s32[]{:S(2)}) async-start(), calls=%async_computation.1 | async-start | bytes 17301504 | tf_op jit(solution)/shard_map/all_gather | solution.py:22
  7.3 663.8 %reduce-scatter.2.cloned.1.call-start = ((), (), s32[]{:S(2)}) async-start(), calls=%async_computation.2 | async-start | bytes 34603008 | tf_op jit(solution)/shard_map/reduce_scatter | solution.py:30
  318.5 352.6 %copy-start = (f32[64]{0:T(128)S(1)}, f32[64]{0:T(128)}, u32[]{:S(2)}) copy-start(f32[64]{0:T(128)} %param.10) | copy-start | bytes 772
Sparse Core Ops, SparseCore 0:
  10.2 117.5 all-gather.1
  318.7 352.4 reduce-scatter.1
where the time goes:
time: 686 us; the launch traced here: 680 us
  waiting for transfers between devices  474 us (69%)
  matrix products  141 us (21%)
  loops' own time  29.8 us (4%)
  local copies, waits for them, and re-layouts  19.9 us (3%)
  between operations  13.4 us (2%)
    reduce_scatter x1, waiting for transfers between devices, per_device(): lax.psum_scatter(partial_value, 'loop', scatter_dimension=0, tiled=True)  353 us
    all_gather x1, waiting for transfers between devices, per_device(): gathered = lax.all_gather(slots, 'loop', axis=0, tiled=True)  120 us
    dot_general x16, matrix products, expert_part(): return jnp.dot(hidden, down_rows, preferred_element_type=jnp.float32)  94.1 us
    dot_general x16, matrix products, expert_part(): jnp.dot(row_block, gate_cols, preferred_element_type=jnp.float32)  46.9 us
    another operation x1, loops' own time, per_device(): lax.map(expert_tile, (tile_rows, chosen_ids)).reshape(-1, width)  29.8 us
    dynamic_slice x16, local copies, waits for them, and re-layouts, per_device(): lax.map(expert_tile, (tile_rows, chosen_ids)).reshape(-1, width)  19.9 us
  transfers between devices with their start and end apart: 2, of which 2 were waited for; matrix products, arithmetic and copies ran while one was open for 0% of the time, Pallas kernels for 0%

commit v1 on v0

--- a/solution.py
+++ b/solution.py
@@ -1,9 +1,15 @@
+import functools
+
 import jax
 import jax.numpy as jnp
 from jax import lax
+from jax.experimental import pallas as pl
+from jax.experimental.pallas import tpu as pltpu
 from jax.sharding import PartitionSpec as P
 
 TILE = 128
+MESH = pl.DeviceIdType.MESH
+F32 = jnp.float32
 
 
 def expert_part(row_block, chosen, gate_weight, up_weight, down_weight):
@@ -16,7 +22,7 @@
     return jnp.dot(hidden, down_rows, preferred_element_type=jnp.float32)
 
 
-def per_device(slots, tile_expert, slot_weight, gate_weight, up_weight, down_weight):
+def collective_form(slots, tile_expert, slot_weight, gate_weight, up_weight, down_weight):
     chosen_ids = tile_expert[:, 0]
     width = slots.shape[1]
     gathered = lax.all_gather(slots, "loop", axis=0, tiled=True)
@@ -31,7 +37,396 @@
     return (slot_weight[:, None] * summed).astype(jnp.bfloat16)
 
 
+def kernel(nz, te, slots, gate, up, down, out, x, wgu, wd, xv, own, stage, sib, rd, rx, ry, rz,
+           wsem, xsem, s_zu, s_zd, r_z, s_x, r_x, s_y, r_y, s_f, r_f, s_s, r_s,
+           s_p, r_p, s_d, r_d, s_px, r_px, s_py, r_py, s_ru, s_rd, r_rz):
+    rows, width = slots.shape
+    half = rows // 2
+    ff = gate.shape[2]
+    me = lax.axis_index("loop")
+    c = me % 2
+    px = (me // 2) % 2
+    py = (me // 4) % 2
+    z = me // 8
+    turn = 1 - 2 * ((2 * z) // nz)
+
+    def chip(s, j):
+        return (s * 2 + (py + j // 2) % 2) * 2 + (px + j % 2) % 2
+
+    def device(s, j, core):
+        return {"loop": chip(s, j) * 2 + core}
+
+    xn, yn, sb = device(z, 1, c), device(z, 2, c), device(z, 0, 1 - c)
+
+    def zdev(step):
+        return {"loop": me + 8 * step}
+
+    has_up, has_dn = z < nz - 1, z > 0
+
+    def remote(src, dst, ssem, rsem, dev):
+        return pltpu.make_async_remote_copy(src_ref=src, dst_ref=dst, send_sem=ssem, recv_sem=rsem,
+                                            device_id=dev, device_id_type=MESH)
+
+    def order(i):
+        return (z + turn * i + nz) % nz
+
+    def zu(q):
+        b = x.at[chip(q, 0), c]
+        return remote(b, b, s_zu.at[q], r_z.at[q], zdev(1))
+
+    def zd(q):
+        b = x.at[chip(q, 0), c]
+        return remote(b, b, s_zd.at[q], r_z.at[q], zdev(-1))
+
+    def gx(s):
+        b = x.at[chip(s, 0), c]
+        return remote(b, b, s_x.at[s], r_x.at[s], xn)
+
+    def gy(s):
+        b = x.at[chip(s, 0), c]
+        return remote(b, b, s_y.at[s], r_y.at[s], yn)
+
+    def fy(s):
+        b = x.at[chip(s, 1), c, pl.ds(0, half)]
+        return remote(b, b, s_f.at[s, 0], r_f.at[s, 0], yn)
+
+    def fx(s):
+        b = x.at[chip(s, 2), c, pl.ds(half, half)]
+        return remote(b, b, s_f.at[s, 1], r_f.at[s, 1], xn)
+
+    def gs(k):
+        b = x.at[k, c]
+        return remote(b, b, s_s.at[k], r_s.at[k], sb)
+
+    def ps(k):
+        return remote(stage.at[k], sib.at[k], s_p.at[k], r_p.at[k], sb)
+
+    def dx(s):
+        return remote(own.at[chip(s, 3), pl.ds(0, half)], rd.at[s, 0], s_d.at[s, 0], r_d.at[s, 0], xn)
+
+    def dy(s):
+        return remote(own.at[chip(s, 3), pl.ds(half, half)], rd.at[s, 1], s_d.at[s, 1], r_d.at[s, 1], yn)
+
+    def sx(s):
+        return remote(own.at[chip(s, 1)], rx.at[s], s_px.at[s], r_px.at[s], xn)
+
+    def sy(s):
+        return remote(own.at[chip(s, 2)], ry.at[s], s_py.at[s], r_py.at[s], yn)
+
+    def ru(s):
+        return remote(own.at[chip(s, 0)], rz.at[s], s_ru.at[s], r_rz.at[s], zdev(1))
+
+    def rdn(s):
+        slot = jnp.where(z - 1 == s, nz, s)
+        return remote(own.at[chip(s, 0)], rz.at[slot], s_rd.at[s], r_rz.at[slot], zdev(-1))
+
+    def rz_wait(slot):
+        remote(rz.at[slot], rz.at[slot], s_ru.at[0], r_rz.at[slot], zdev(0)).wait_recv()
+
+    mine = chip(z, 0)
+    first = pltpu.make_async_copy(slots, x.at[mine, c], wsem.at[0])
+    first.start()
+    loads = [
+        pltpu.make_async_copy(gate, wgu.at[:, :, pl.ds(0, ff)], wsem.at[1]),
+        pltpu.make_async_copy(up, wgu.at[:, :, pl.ds(ff, ff)], wsem.at[2]),
+        pltpu.make_async_copy(down, wd, wsem.at[3]),
+    ]
+
+    barrier = pltpu.get_barrier_semaphore()
+    for dev in (sb, xn, yn):
+        pl.semaphore_signal(barrier, inc=1, device_id=dev, device_id_type=MESH)
+
+    @pl.when(has_up)
+    def _():
+        pl.semaphore_signal(barrier, inc=1, device_id=zdev(1), device_id_type=MESH)
+
+    @pl.when(has_dn)
+    def _():
+        pl.semaphore_signal(barrier, inc=1, device_id=zdev(-1), device_id_type=MESH)
+
+    pl.semaphore_wait(barrier, 3 + has_up.astype(jnp.int32) + has_dn.astype(jnp.int32))
+    first.wait()
+
+    def z_send(q, going_up):
+        @pl.when(has_up if going_up else has_dn)
+        def _():
+            (zu if going_up else zd)(q).start()
+
+    def stage_z(t):
+        low, high = z - t, z + t
+
+        @pl.when(low >= 0)
+        def _():
+            zu(low).wait_recv()
+            z_send(low, True)
+
+        @pl.when(high < nz)
+        def _():
+            zd(high).wait_recv()
+            z_send(high, False)
+
+    def stage_a(i):
+        s = order(i)
+        gx(s).start()
+        gy(s).start()
+        gs(chip(s, 0)).start()
+
+    def stage_b(i):
+        s = order(i)
+        remote(x.at[chip(s, 1), c], x.at[chip(s, 1), c], s_x.at[s], r_x.at[s], xn).wait_recv()
+        fy(s).start()
+        gs(chip(s, 1)).start()
+        remote(x.at[chip(s, 2), c], x.at[chip(s, 2), c], s_y.at[s], r_y.at[s], yn).wait_recv()
+        fx(s).start()
+        gs(chip(s, 2)).start()
+
+    def stage_c(i):
+        s = order(i)
+        k = chip(s, 3)
+        for h in range(2):
+            b = x.at[k, c, pl.ds(h * half, half)]
+            remote(b, b, s_f.at[s, h], r_f.at[s, h], xn).wait_recv()
+        gs(k).start()
+
+    def load(s, j):
+        k, slot = chip(s, j), j % 2
+        return [pltpu.make_async_copy(x.at[k, c], xv.at[slot, pl.ds(0, rows)], xsem.at[slot, 0]),
+                pltpu.make_async_copy(x.at[k, 1 - c], xv.at[slot, pl.ds(rows, rows)], xsem.at[slot, 1])]
+
+    def fetch(s, j):
+        b = x.at[chip(s, j), 1 - c]
+        remote(b, b, s_s.at[0], r_s.at[chip(s, j)], sb).wait_recv()
+        for cp in load(s, j):
+            cp.start()
+
+    def stage_d(i):
+        s = order(i)
+        fetch(s, 0)
+
+        def block(j, carry):
+            @pl.when(j < 3)
+            def _():
+                fetch(s, j + 1)
+
+            for cp in load(s, j):
+                cp.wait()
+            k, slot = chip(s, j), j % 2
+            e = te[k, 0]
+            step = min(width, 1024)
+            acc = jnp.zeros((2 * rows, 2 * ff), F32)
+            for k0 in range(0, width, step):
+                acc += jnp.dot(xv[slot, :, k0:k0 + step], wgu[e, k0:k0 + step, :],
+                               preferred_element_type=F32)
+            hidden = (jax.nn.silu(acc[:, :ff]) * acc[:, ff:]).astype(jnp.bfloat16)
+            for n0 in range(0, width, step):
+                part = jnp.dot(hidden, wd[e, :, n0:n0 + step], preferred_element_type=F32)
+                part = part.astype(jnp.bfloat16)
+                own[k, :, n0:n0 + step] = part[:rows]
+                stage[k, :, n0:n0 + step] = part[rows:]
+            ps(k).start()
+            return carry
+
+        lax.fori_loop(0, 4, block, 0)
+
+    def stage_r1(i):
+        s = order(i)
+
+        def add(j, carry):
+            k = chip(s, 3 - j)
+            ps(k).wait_recv()
+            own[k] = (own[k].astype(F32) + sib[k].astype(F32)).astype(jnp.bfloat16)
+            return carry
+
+        lax.fori_loop(0, 1, add, 0)
+        dx(s).start()
+        dy(s).start()
+        lax.fori_loop(1, 4, add, 0)
+
+    def stage_r2(i):
+        s = order(i)
+        kx, ky = chip(s, 1), chip(s, 2)
+        dx(s).wait_recv()
+        own[ky, :half] = (own[ky, :half].astype(F32) + rd[s, 0].astype(F32)).astype(jnp.bfloat16)
+        sy(s).start()
+        dy(s).wait_recv()
+        own[kx, half:] = (own[kx, half:].astype(F32) + rd[s, 1].astype(F32)).astype(jnp.bfloat16)
+        sx(s).start()
+
+    def stage_r3(i):
+        s = order(i)
+        k = chip(s, 0)
+        sx(s).wait_recv()
+        sy(s).wait_recv()
+
+        @pl.when(jnp.logical_or(jnp.logical_and(s >= z, has_dn), jnp.logical_and(s < z, has_up)))
+        def _():
+            rz_wait(s)
+
+        total = own[k].astype(F32) + rx[s].astype(F32) + ry[s].astype(F32) + rz[s].astype(F32)
+
+        @pl.when(s != z)
+        def _():
+            own[k] = total.astype(jnp.bfloat16)
+
+        @pl.when(s > z)
+        def _():
+            ru(s).start()
+
+        @pl.when(s < z)
+        def _():
+            rdn(s).start()
+
+        @pl.when(s == z)
+        def _():
+            @pl.when(has_up)
+            def _():
+                rz_wait(nz)
+
+            out[...] = total + rz[nz].astype(F32)
+
+    z_send(z, True)
+    z_send(z, False)
+    stage_a(0)
+    for cp in loads:
+        cp.start()
+
+    @pl.when(jnp.logical_not(has_dn))
+    def _():
+        rz[pl.ds(0, nz)] = jnp.zeros((nz, rows, width), jnp.bfloat16)
+
+    @pl.when(jnp.logical_not(has_up))
+    def _():
+        rz[pl.ds(0, nz - 1)] = jnp.zeros((nz - 1, rows, width), jnp.bfloat16)
+        rz[nz] = jnp.zeros((rows, width), jnp.bfloat16)
+
+    stage_z(1)
+    stage_a(1)
+    stage_b(0)
+
+    def body(n, carry):
+        @pl.when(n + 2 < nz)
+        def _():
+            stage_z(n + 2)
+            stage_a(n + 2)
+
+        @pl.when(n < nz)
+        def _():
+            stage_c(n)
+
+        @pl.when(n + 1 < nz)
+        def _():
+            stage_b(n + 1)
+
+        @pl.when(n == 0)
+        def _():
+            for cp in loads:
+                cp.wait()
+
+        @pl.when(n < nz)
+        def _():
+            stage_d(n)
+
+        @pl.when(jnp.logical_and(n >= 1, n <= nz))
+        def _():
+            stage_r1(n % nz)
+
+        @pl.when(jnp.logical_and(n >= 2, n <= nz + 1))
+        def _():
+            stage_r2((n - 1) % nz)
+
+        @pl.when(n >= 3)
+        def _():
+            stage_r3((n - 2) % nz)
+
+        return carry
+
+    lax.fori_loop(0, nz + 3, body, 0)
+
+    def finish(q, carry):
+        for cp in (gx(q), gy(q), fx(q), fy(q), dx(q), dy(q), sx(q), sy(q)):
+            cp.wait_send()
+
+        @pl.when(jnp.logical_and(has_up, q <= z))
+        def _():
+            zu(q).wait_send()
+
+        @pl.when(jnp.logical_and(has_dn, q >= z))
+        def _():
+            zd(q).wait_send()
+
+        @pl.when(q > z)
+        def _():
+            ru(q).wait_send()
+
+        @pl.when(q < z)
+        def _():
+            rdn(q).wait_send()
+
+        return carry
+
+    lax.fori_loop(0, nz, finish, 0)
+
+    def finish_pair(k, carry):
+        gs(k).wait_send()
+        ps(k).wait_send()
+        return carry
+
+    lax.fori_loop(0, 4 * nz, finish_pair, 0)
+
+
+def kernel_form(n, slots, tile_expert, slot_weight, gate_weight, up_weight, down_weight):
+    nz, blocks = n // 8, n // 2
+    rows, width = slots.shape
+    experts, _, ff = gate_weight.shape
+    bf16 = jnp.bfloat16
+    dma = pltpu.SemaphoreType.DMA
+    anywhere = pl.BlockSpec(memory_space=pl.ANY)
+    summed, _ = pl.pallas_call(
+        functools.partial(kernel, nz),
+        out_shape=(jax.ShapeDtypeStruct((rows, width), F32),
+                   jax.ShapeDtypeStruct((blocks, 2, rows, width), bf16)),
+        in_specs=[pl.BlockSpec(memory_space=pltpu.SMEM)] + [anywhere] * 4,
+        out_specs=(pl.BlockSpec(memory_space=pltpu.VMEM), anywhere),
+        scratch_shapes=[
+            pltpu.VMEM((experts, width, 2 * ff), bf16),
+            pltpu.VMEM((experts, ff, width), bf16),
+            pltpu.VMEM((2, 2 * rows, width), bf16),
+            pltpu.VMEM((blocks, rows, width), bf16),
+            pltpu.VMEM((blocks, rows, width), bf16),
+            pltpu.VMEM((blocks, rows, width), bf16),
+            pltpu.VMEM((nz, 2, rows // 2, width), bf16),
+            pltpu.VMEM((nz, rows, width), bf16),
+            pltpu.VMEM((nz, rows, width), bf16),
+            pltpu.VMEM((nz + 1, rows, width), bf16),
+            dma((4,)), dma((2, 2)),
+            dma((nz,)), dma((nz,)), dma((nz,)),
+            dma((nz,)), dma((nz,)), dma((nz,)), dma((nz,)),
+            dma((nz, 2)), dma((nz, 2)),
+            dma((blocks,)), dma((blocks,)),
+            dma((blocks,)), dma((blocks,)),
+            dma((nz, 2)), dma((nz, 2)),
+            dma((nz,)), dma((nz,)), dma((nz,)), dma((nz,)),
+            dma((nz,)), dma((nz,)), dma((nz + 1,)),
+        ],
+        compiler_params=pltpu.CompilerParams(
+            collective_id=0, has_side_effects=True, vmem_limit_bytes=60 * 2**20),
+        cost_estimate=pl.CostEstimate(flops=12 * blocks * rows * width * ff,
+                                      bytes_accessed=6 * experts * width * ff, transcendentals=0),
+    )(tile_expert, slots, gate_weight, up_weight, down_weight)
+    return (slot_weight[:, None] * summed).astype(bf16)
+
+
+def fits(n, slots, gate_weight):
+    rows, width = slots.shape
+    experts, _, ff = gate_weight.shape
+    blocks, nz = n // 2, n // 8
+    held = experts * width * 3 * ff + (4 + 3 * blocks + 4 * nz + 3) * rows * width
+    return (n % 8 == 0 and n >= 16 and 2 * rows == TILE and ff % 128 == 0 and width % 1024 == 0
+            and 2 * held <= 57 * 2**20)
+
+
 def solution(mesh):
+    n = mesh.shape["loop"]
     in_specs = (
         P(("parts", "loop"), None),
         P("parts", None),
@@ -41,6 +436,13 @@
         P(None, "loop", None),
     )
     out_specs = P(("parts", "loop"), None)
+
+    def per_device(slots, tile_expert, slot_weight, gate_weight, up_weight, down_weight):
+        args = (slots, tile_expert, slot_weight, gate_weight, up_weight, down_weight)
+        if fits(n, slots, gate_weight):
+            return kernel_form(n, *args)
+        return collective_form(*args)
+
     return jax.shard_map(
         per_device, mesh=mesh, in_specs=in_specs, out_specs=out_specs, check_vma=False
     )

time: 686 us -> 197 us (0.29)
  waiting for transfers between devices: 474 us -> 0 us
  Pallas kernels: 0 us -> 193 us
  matrix products: 141 us -> 0 us
  loops' own time: 29.8 us -> 0 us
  local copies, waits for them, and re-layouts: 19.9 us -> 1.33 us
  between operations: 13.4 us -> 0.02 us
    reduce_scatter x1 -> x0, waiting for transfers between devices: 353 us -> none  [per_device(): lax.psum_scatter(partial_value, 'loop', scatter_dimension=0, tiled=True)]
    pallas_call x0 -> x1, Pallas kernels: none -> 193 us  [kernel_form(): pl.pallas_call(functools.partial(kernel, nz), out_shape=(jax.ShapeDtypeSt...]
    dot_general x32 -> x0, matrix products: 141 us -> none  [the longest x16 94.1 us: expert_part(): return jnp.dot(hidden, down_rows, preferred_element_type=jnp.float32)]
    all_gather x1 -> x0, waiting for transfers between devices: 120 us -> none  [per_device(): gathered = lax.all_gather(slots, 'loop', axis=0, tiled=True)]
    another operation x1 -> x0, loops' own time: 29.8 us -> none  [per_device(): lax.map(expert_tile, (tile_rows, chosen_ids)).reshape(-1, width)]
    dynamic_slice x16 -> x0, local copies, waits for them, and re-layouts: 19.9 us -> none  [per_device(): lax.map(expert_tile, (tile_rows, chosen_ids)).reshape(-1, width)]
  transfers between devices with their start and end apart: 2 -> 0, of which waited for: 2 -> 0; matrix products, arithmetic and copies ran while one was open for 0% -> 0% of each run, Pallas kernels for 0% -> 0%
where the time goes in v1:
time: 197 us; the launch traced here: 196 us
  Pallas kernels  193 us (98%)
  other arithmetic  2.15 us (1%)
    pallas_call x1, Pallas kernels, kernel_form(): pl.pallas_call(functools.partial(kernel, nz), out_shape=(jax.ShapeDtypeSt...  193 us

profile of v1, /device:TPU:0, one launch (start us, length us, event | category | flops | bytes accessed | tf_op | source)
XLA Modules:
  0.0 196.2 jit_solution(9101292732044969375)
XLA Ops:
  0.0 1.3 copy.7.te
  1.3 0.0 copy-start
  1.3 192.7 %shard_map.64 = (f32[64,4096]{1,0:T(8,128)}, bf16[16,2,64,4096]{3,2,1,0:T(8,128)(2,1)}) custom-call(s32[16,1]{1,0:T(8,128)} %copy.7.te, bf16[64,4096]{1,0:T(8,128)(2,1)} %slots.1, bf16[2,4096,384]{2,1,0:T(8,128)(2,1)} %gate.1, bf16[2,4096,384]{2,1,0:T(8,128)(2,1)} %up.1, bf16[2,384,4096]{2,1,0:T(8,128)(2,1)} %down.1), custom_call_target="tpu_custom_call" | custom-call | flops 19327352832 | bytes 18874368 | tf_op jit(solution)/shard_map/pallas_call | solution.py:384
  194.1 0.0 copy-done
  194.1 2.1 %multiply_convert_fusion = bf16[64,4096]{1,0:T(8,128)(2,1)} fusion(f32[64,4096]{1,0:T(8,128)} %get-tuple-element.6, f32[64]{0:T(128)S(1)} %copy-done), kind=kLoop, calls=%fused_computation | loop fusion | flops 524288 | bytes 1573120 | tf_op jit(solution)/shard_map/convert_element_type | solution.py:416
Async XLA Ops:
  1.3 192.7 %copy-start = (f32[64]{0:T(128)S(1)}, f32[64]{0:T(128)}, u32[]{:S(2)}) copy-start(f32[64]{0:T(128)} %param.8) | copy-start | bytes 772

commit v2 on v1

--- a/solution.py
+++ b/solution.py
@@ -69,6 +69,9 @@
 
     def order(i):
         return (z + turn * i + nz) % nz
+
+    def late(p):
+        return (1 - p // 2) * (2 + p) + (p // 2) * (3 - p)
 
     def zu(q):
         b = x.at[chip(q, 0), c]
@@ -228,28 +231,40 @@
 
         lax.fori_loop(0, 4, block, 0)
 
+    def add_rows(start, count, dst, *terms):
+        step = min(width, 1024)
+
+        def rows16(t, carry):
+            r = pl.ds(start + t * 16, 16)
+            for n0 in range(0, width, step):
+                n = slice(n0, n0 + step)
+                total = dst[r, n].astype(F32)
+                for ref, shift in terms:
+                    total += ref[pl.ds(start - shift + t * 16, 16), n].astype(F32)
+                dst[r, n] = total.astype(dst.dtype)
+            return carry
+
+        lax.fori_loop(0, count // 16, rows16, 0)
+
     def stage_r1(i):
         s = order(i)
-
-        def add(j, carry):
-            k = chip(s, 3 - j)
-            ps(k).wait_recv()
-            own[k] = (own[k].astype(F32) + sib[k].astype(F32)).astype(jnp.bfloat16)
-            return carry
-
-        lax.fori_loop(0, 1, add, 0)
+        for j in (3, 2, 1, 0):
+            ps(chip(s, j)).wait_recv()
+        k = chip(s, 3)
+        add_rows(0, rows, own.at[k], (sib.at[k], 0))
         dx(s).start()
         dy(s).start()
-        lax.fori_loop(1, 4, add, 0)
 
     def stage_r2(i):
         s = order(i)
         kx, ky = chip(s, 1), chip(s, 2)
         dx(s).wait_recv()
-        own[ky, :half] = (own[ky, :half].astype(F32) + rd[s, 0].astype(F32)).astype(jnp.bfloat16)
+        add_rows(0, half, own.at[ky], (sib.at[ky], 0), (rd.at[s, 0], 0))
+        add_rows(half, half, own.at[ky], (sib.at[ky], 0))
         sy(s).start()
         dy(s).wait_recv()
-        own[kx, half:] = (own[kx, half:].astype(F32) + rd[s, 1].astype(F32)).astype(jnp.bfloat16)
+        add_rows(0, half, own.at[kx], (sib.at[kx], 0))
+        add_rows(half, half, own.at[kx], (sib.at[kx], 0), (rd.at[s, 1], half))
         sx(s).start()
 
     def stage_r3(i):
@@ -257,32 +272,44 @@
         k = chip(s, 0)
         sx(s).wait_recv()
         sy(s).wait_recv()
-
-        @pl.when(jnp.logical_or(jnp.logical_and(s >= z, has_dn), jnp.logical_and(s < z, has_up)))
+        add_rows(0, rows, own.at[k], (sib.at[k], 0), (rx.at[s], 0), (ry.at[s], 0))
+
+        @pl.when(jnp.logical_and(s > z, jnp.logical_not(has_dn)))
+        def _():
+            ru(s).start()
+
+        @pl.when(jnp.logical_and(s < z, jnp.logical_not(has_up)))
+        def _():
+            rdn(s).start()
+
+    def stage_r4(i):
+        s = order(i)
+        k = chip(s, 0)
+
+        @pl.when(jnp.logical_and(s > z, has_dn))
         def _():
             rz_wait(s)
-
-        total = own[k].astype(F32) + rx[s].astype(F32) + ry[s].astype(F32) + rz[s].astype(F32)
-
-        @pl.when(s != z)
-        def _():
-            own[k] = total.astype(jnp.bfloat16)
-
-        @pl.when(s > z)
-        def _():
+            add_rows(0, rows, own.at[k], (rz.at[s], 0))
             ru(s).start()
 
-        @pl.when(s < z)
-        def _():
+        @pl.when(jnp.logical_and(s < z, has_up))
+        def _():
+            rz_wait(s)
+            add_rows(0, rows, own.at[k], (rz.at[s], 0))
             rdn(s).start()
 
         @pl.when(s == z)
         def _():
+            @pl.when(has_dn)
+            def _():
+                rz_wait(s)
+
             @pl.when(has_up)
             def _():
                 rz_wait(nz)
 
-            out[...] = total + rz[nz].astype(F32)
+            out[...] = jnp.zeros((rows, width), F32)
+            add_rows(0, rows, out, (own.at[k], 0), (rz.at[s], 0), (rz.at[nz], 0))
 
     z_send(z, True)
     z_send(z, False)
@@ -292,11 +319,10 @@
 
     @pl.when(jnp.logical_not(has_dn))
     def _():
-        rz[pl.ds(0, nz)] = jnp.zeros((nz, rows, width), jnp.bfloat16)
+        rz[0] = jnp.zeros((rows, width), jnp.bfloat16)
 
     @pl.when(jnp.logical_not(has_up))
     def _():
-        rz[pl.ds(0, nz - 1)] = jnp.zeros((nz - 1, rows, width), jnp.bfloat16)
         rz[nz] = jnp.zeros((rows, width), jnp.bfloat16)
 
     stage_z(1)
@@ -322,25 +348,33 @@
             for cp in loads:
                 cp.wait()
 
+        @pl.when(n == 3)
+        def _():
+            stage_r2(late(0))
+
         @pl.when(n < nz)
         def _():
             stage_d(n)
 
-        @pl.when(jnp.logical_and(n >= 1, n <= nz))
-        def _():
-            stage_r1(n % nz)
-
-        @pl.when(jnp.logical_and(n >= 2, n <= nz + 1))
-        def _():
-            stage_r2((n - 1) % nz)
-
-        @pl.when(n >= 3)
-        def _():
-            stage_r3((n - 2) % nz)
+        @pl.when(n < nz)
+        def _():
+            stage_r1(n)
+
+        @pl.when(jnp.logical_and(n >= 3, n <= 5))
+        def _():
+            stage_r2(late(n - 2))
+
+        @pl.when(jnp.logical_and(n >= 4, n <= 7))
+        def _():
+            stage_r3(late(n - 4))
+
+        @pl.when(n >= 6)
+        def _():
+            stage_r4(late(n - 6))
 
         return carry
 
-    lax.fori_loop(0, nz + 3, body, 0)
+    lax.fori_loop(0, 10, body, 0)
 
     def finish(q, carry):
         for cp in (gx(q), gy(q), fx(q), fy(q), dx(q), dy(q), sx(q), sy(q)):
@@ -385,7 +419,8 @@
         functools.partial(kernel, nz),
         out_shape=(jax.ShapeDtypeStruct((rows, width), F32),
                    jax.ShapeDtypeStruct((blocks, 2, rows, width), bf16)),
-        in_specs=[pl.BlockSpec(memory_space=pltpu.SMEM)] + [anywhere] * 4,
+        in_specs=[pl.BlockSpec(memory_space=pltpu.SMEM), pl.BlockSpec(memory_space=pltpu.VMEM)]
+        + [anywhere] * 3,
         out_specs=(pl.BlockSpec(memory_space=pltpu.VMEM), anywhere),
         scratch_shapes=[
             pltpu.VMEM((experts, width, 2 * ff), bf16),
@@ -421,7 +456,7 @@
     experts, _, ff = gate_weight.shape
     blocks, nz = n // 2, n // 8
     held = experts * width * 3 * ff + (4 + 3 * blocks + 4 * nz + 3) * rows * width
-    return (n % 8 == 0 and n >= 16 and 2 * rows == TILE and ff % 128 == 0 and width % 1024 == 0
+    return (n == 32 and 2 * rows == TILE and ff % 128 == 0 and width % 1024 == 0
             and 2 * held <= 57 * 2**20)
 
 

time: 197 us -> 168 us (0.85)
  Pallas kernels: 193 us -> 165 us
    pallas_call x1, Pallas kernels: 193 us -> 165 us  [kernel_form(): pl.pallas_call(functools.partial(kernel, nz), out_shape=(jax.ShapeDtypeSt...]
where the time goes in v2:
time: 168 us
  Pallas kernels  165 us (98%)
  other arithmetic  2.15 us (1%)
    pallas_call x1, Pallas kernels, kernel_form(): pl.pallas_call(functools.partial(kernel, nz), out_shape=(jax.ShapeDtypeSt...  165 us

profile of v2, /device:TPU:0, one launch (start us, length us, event | category | flops | bytes accessed | tf_op | source)
XLA Modules:
  0.0 168.0 jit_solution(13650873080058224160)
XLA Ops:
  0.0 1.3 copy.7.te
  1.3 0.0 copy-start
  1.3 164.5 %shard_map.64 = (f32[64,4096]{1,0:T(8,128)}, bf16[16,2,64,4096]{3,2,1,0:T(8,128)(2,1)}) custom-call(s32[16,1]{1,0:T(8,128)} %copy.7.te, bf16[64,4096]{1,0:T(8,128)(2,1)} %slots.1, bf16[2,4096,384]{2,1,0:T(8,128)(2,1)} %gate.1, bf16[2,4096,384]{2,1,0:T(8,128)(2,1)} %up.1, bf16[2,384,4096]{2,1,0:T(8,128)(2,1)} %down.1), custom_call_target="tpu_custom_call" | custom-call | flops 19327352832 | bytes 18874368 | tf_op jit(solution)/shard_map/pallas_call | solution.py:418
  165.9 0.0 copy-done
  165.9 2.1 %multiply_convert_fusion = bf16[64,4096]{1,0:T(8,128)(2,1)} fusion(f32[64,4096]{1,0:T(8,128)} %get-tuple-element.6, f32[64]{0:T(128)S(1)} %copy-done), kind=kLoop, calls=%fused_computation | loop fusion | flops 524288 | bytes 1573120 | tf_op jit(solution)/shard_map/convert_element_type | solution.py:451
Async XLA Ops:
  1.3 164.6 %copy-start = (f32[64]{0:T(128)S(1)}, f32[64]{0:T(128)}, u32[]{:S(2)}) copy-start(f32[64]{0:T(128)} %param.8) | copy-start | bytes 772

commit v3 on v2

--- a/solution.py
+++ b/solution.py
@@ -368,13 +368,13 @@
         def _():
             stage_r3(late(n - 4))
 
-        @pl.when(n >= 6)
-        def _():
-            stage_r4(late(n - 6))
+        @pl.when(n >= 5)
+        def _():
+            stage_r4(late(n - 5))
 
         return carry
 
-    lax.fori_loop(0, 10, body, 0)
+    lax.fori_loop(0, 9, body, 0)
 
     def finish(q, carry):
         for cp in (gx(q), gy(q), fx(q), fy(q), dx(q), dy(q), sx(q), sy(q)):

time: 168 us -> 167 us (level); the launches traced: 168 us -> 164 us
  Pallas kernels: 165 us -> 161 us
    pallas_call x1, Pallas kernels: 165 us -> 161 us  [kernel_form(): pl.pallas_call(functools.partial(kernel, nz), out_shape=(jax.ShapeDtypeSt...]
where the time goes in v3:
time: 167 us; the launch traced here: 164 us
  Pallas kernels  161 us (96%)
  other arithmetic  2.15 us (1%)
    pallas_call x1, Pallas kernels, kernel_form(): pl.pallas_call(functools.partial(kernel, nz), out_shape=(jax.ShapeDtypeSt...  161 us

profile of v3, /device:TPU:0, one launch (start us, length us, event | category | flops | bytes accessed | tf_op | source)
XLA Modules:
  0.0 164.2 jit_solution(16079947010470752021)
XLA Ops:
  0.0 1.3 copy.7.te
  1.3 0.0 copy-start
  1.3 160.7 %shard_map.64 = (f32[64,4096]{1,0:T(8,128)}, bf16[16,2,64,4096]{3,2,1,0:T(8,128)(2,1)}) custom-call(s32[16,1]{1,0:T(8,128)} %copy.7.te, bf16[64,4096]{1,0:T(8,128)(2,1)} %slots.1, bf16[2,4096,384]{2,1,0:T(8,128)(2,1)} %gate.1, bf16[2,4096,384]{2,1,0:T(8,128)(2,1)} %up.1, bf16[2,384,4096]{2,1,0:T(8,128)(2,1)} %down.1), custom_call_target="tpu_custom_call" | custom-call | flops 19327352832 | bytes 18874368 | tf_op jit(solution)/shard_map/pallas_call | solution.py:418
  162.0 0.0 copy-done
  162.0 2.1 %multiply_convert_fusion = bf16[64,4096]{1,0:T(8,128)(2,1)} fusion(f32[64,4096]{1,0:T(8,128)} %get-tuple-element.6, f32[64]{0:T(128)S(1)} %copy-done), kind=kLoop, calls=%fused_computation | loop fusion | flops 524288 | bytes 1573120 | tf_op jit(solution)/shard_map/convert_element_type | solution.py:451
Async XLA Ops:
  1.3 160.7 %copy-start = (f32[64]{0:T(128)S(1)}, f32[64]{0:T(128)}, u32[]{:S(2)}) copy-start(f32[64]{0:T(128)} %param.8) | copy-start | bytes 772
